TPU v7x, 32 devices: a whole 2x2x4 slice. The times are simulated.
32 devices in a mesh: groups: 2 (over y), front: 4 (over z), batch: 2 (over x), line: 2 (over core).
Axes of the slice: x: 2, y: 2, z: 4, core: 2. Of those that a mesh axis runs over, the one named last changes fastest.
Arguments:
- injections: float32 [2048, 512], P('front', ('groups', 'batch')), parts along dimension 1, may hold values from -6 to 6
- switch_from: int32 [2, 512], P(None, ('groups', 'batch')), parts along dimension 1, may hold values from 0 to 2047
- switch_to: int32 [2, 512], P(None, ('groups', 'batch')), parts along dimension 1, may hold values from 0 to 2047
- switch_susc: float32 [2, 512], P(None, ('groups', 'batch')), parts along dimension 1, may hold values from 0.5 to 4
- coupling: float32 [2048, 512], P('front'), may hold values from -1 to 1
- pivot_inverse: float32 [2048, 512], P('front')
- branch_from: int32 [4096], P(('front', 'line')), may hold values from 0 to 2047, as said below
- branch_to: int32 [4096], P(('front', 'line')), may hold values from 0 to 2047, as said below
- branch_susc: float32 [4096], P(('front', 'line')), may hold values from 0.5 to 2
- branch_owner: int32 [4096, 1], P(('front', 'line')), may hold values from 0 to 7; in each aligned block of 512 rows (0 to 511, 512 to 1023, ...) at most 128 rows name the same one
- in_weight: float32 [128], replicated, may hold values from -4 to 4
- in_bias: float32 [128], replicated, may hold values from -1 to 1
- out_weight: bfloat16 [128, 128], replicated, may hold values from -0.5 to 0.5
Outputs:
- region_scores: bfloat16 [8, 512, 128], P(('front', 'line'), ('groups', 'batch')), parts along dimension 1
- angles: float32 [2048, 512], P('front', ('groups', 'batch')), parts along dimension 1
There are 2 independent parts, one for each index of `groups`. A program takes and returns all parts, laid end to end along the dimension named above; an argument that names none is the same for every part. Nothing has to cross between parts.
Inputs may be any that keep to these rules, and one draw needn't show every extreme that they name: `branch_from`: the bus of row r lies in slab s = r // 1024, between s * 512 and s * 512 + 511. `branch_to`: the bus of row r lies in slab s = r // 1024 or in slab s + 1. `branch_owner`: in each aligned block of 512 rows (the branches of one device) no owner is named by more than 128 rows.
All inputs are finite; a program needn't handle non-finite values.
Results may differ from a plain program's by a relative error of at most 0.005.
Values sent between devices are 32-bit elements; how exact they have to be, the bound alone decides.
A program may use at most 64 MiB of HBM per device.

v0:
```python
import jax
import jax.numpy as jnp
from jax import lax
from jax.sharding import PartitionSpec as P

K = 2
BR_DEV = 512


def from_behind(value, axis, by):
    count = lax.axis_size(axis)
    pairs = [(i, i + by) for i in range(count) if 0 <= i + by < count]
    return lax.ppermute(value, axis, pairs)


def product(operand, against):
    return jnp.dot(
        operand, against, precision=lax.Precision.HIGHEST, preferred_element_type=jnp.float32
    )


def centered_tanh(loadings, in_weight, in_bias):
    return jnp.tanh(loadings[..., None] * in_weight + in_bias) - jnp.tanh(in_bias)


def capacitance_solve(terms, switch_susc):
    switches = switch_susc.shape[0]
    factor = [[None] * switches for row_at in range(switches)]
    for row_at in range(switches):
        for col_at in range(row_at + 1):
            partial_sum = terms[row_at, 1 + col_at]
            if row_at == col_at:
                partial_sum = partial_sum + 1.0 / switch_susc[row_at]
            for inner_at in range(col_at):
                partial_sum = partial_sum - factor[row_at][inner_at] * factor[col_at][inner_at]
            if row_at == col_at:
                factor[row_at][col_at] = jnp.sqrt(partial_sum)
            else:
                factor[row_at][col_at] = partial_sum / factor[col_at][col_at]
    lower_part = []
    for row_at in range(switches):
        running = terms[row_at, 0]
        for inner_at in range(row_at):
            running = running - factor[row_at][inner_at] * lower_part[inner_at]
        lower_part.append(running / factor[row_at][row_at])
    weights = [None] * switches
    for row_at in reversed(range(switches)):
        running = lower_part[row_at]
        for inner_at in range(row_at + 1, switches):
            running = running - factor[inner_at][row_at] * weights[inner_at]
        weights[row_at] = running / factor[row_at][row_at]
    return jnp.stack(weights)


def body(
    injections,
    switch_from,
    switch_to,
    switch_susc,
    coupling,
    pivot_inverse,
    branch_from,
    branch_to,
    branch_susc,
    branch_owner,
    in_weight,
    in_bias,
    out_weight,
):
    fronts = lax.axis_size("front")
    front_at = lax.axis_index("front")
    slab_size = coupling.shape[1]
    topo_count = injections.shape[1]
    first_bus = front_at * slab_size
    bus_ids = first_bus + jnp.arange(slab_size, dtype=jnp.int32)
    from_hot = (bus_ids[:, None, None] == switch_from[None]).astype(jnp.float32)
    to_hot = (bus_ids[:, None, None] == switch_to[None]).astype(jnp.float32)
    incidence = from_hot - to_hot
    stacked = jnp.concatenate([injections[:, None, :], incidence], axis=1).reshape(slab_size, -1)

    def lower_step(step_at, current):
        arrived = from_behind(current, "front", 1)
        return stacked - product(coupling, arrived)

    lowered = lax.fori_loop(0, fronts - 1, lower_step, stacked)
    pivoted = product(pivot_inverse, lowered)

    def upper_step(step_at, current):
        arrived = from_behind(product(coupling.T, current), "front", -1)
        return pivoted - arrived

    solved = lax.fori_loop(0, fronts - 1, upper_step, pivoted)
    solved_cols = solved.reshape(slab_size, K + 1, topo_count)
    local_terms = jnp.einsum(
        "bit,bct->ict", incidence, solved_cols, precision=lax.Precision.HIGHEST
    )
    terms = lax.psum(local_terms, "front")
    weights = capacitance_solve(terms, switch_susc)
    angles = solved_cols[:, 0, :] - jnp.einsum(
        "bit,it->bt", solved_cols[:, 1:, :], weights, precision=lax.Precision.HIGHEST
    )
    following = from_behind(angles, "front", -1)
    joined = jnp.concatenate([angles, following], axis=0)
    flows = branch_susc[:, None] * (joined[branch_from - first_bus] - joined[branch_to - first_bus])
    owners = lax.axis_size(("front", "line"))
    capacity = 2 * BR_DEV // owners
    owner_ids = branch_owner[:, 0]
    owner_hot = (owner_ids[:, None] == jnp.arange(owners, dtype=jnp.int32)[None]).astype(jnp.int32)
    before = jnp.cumsum(owner_hot, axis=0) - owner_hot
    position = jnp.sum(before * owner_hot, axis=1)
    slot_ids = owner_ids * capacity + position
    dispatch = (jnp.arange(owners * capacity, dtype=jnp.int32)[:, None] == slot_ids[None]).astype(
        jnp.float32
    )
    outgoing = product(dispatch, flows).reshape(owners, capacity, topo_count)
    arrived = lax.all_to_all(outgoing, ("front", "line"), split_axis=0, concat_axis=0, tiled=True)
    slot_rows = arrived.reshape(-1, arrived.shape[2])
    span_size = 32
    blocks = slot_rows.reshape(-1, span_size, slot_rows.shape[1])

    def accumulate(running, slot_block):
        return (running + jnp.sum(centered_tanh(slot_block, in_weight, in_bias), axis=0), None)

    start_sum = jnp.zeros((slot_rows.shape[1], in_weight.shape[0]), jnp.float32)
    summed, unused = lax.scan(accumulate, start_sum, blocks)
    pooled = (summed * BR_DEV ** (-0.5)).astype(jnp.bfloat16)
    region_scores = jnp.dot(pooled, out_weight, preferred_element_type=jnp.float32).astype(
        jnp.bfloat16
    )
    return (region_scores[None], angles)


def solution(mesh):
    in_specs = (
        P("front", ("groups", "batch")),
        P(None, ("groups", "batch")),
        P(None, ("groups", "batch")),
        P(None, ("groups", "batch")),
        P("front", None),
        P("front", None),
        P(("front", "line")),
        P(("front", "line")),
        P(("front", "line")),
        P(("front", "line"), None),
        P(),
        P(),
        P(),
    )
    out_specs = (P(("front", "line"), ("groups", "batch"), None), P("front", ("groups", "batch")))
    return jax.shard_map(body, mesh=mesh, in_specs=in_specs, out_specs=out_specs, check_vma=False)
```

profile of v0, /device:TPU:0, one launch (start us, length us, event | category | flops | bytes accessed | tf_op | source)
XLA Modules:
  0.0 243.3 jit_solution(18174583019754320143)
XLA Ops:
  4.5 73.9 %while.32 = (s32[]{:T(128)}, f32[512,384]{1,0:T(8,128)}, f32[512,512]{1,0:T(8,128)S(1)}, f32[512,384]{1,0:T(8,128)S(1)}, s32[]{:T(128)}) while((s32[]{:T(128)}, f32[512,384]{1,0:T(8,128)}, f32[512,512]{1,0:T(8,128)S(1)}, f32[512,384]{1,0:T(8,128)S(1)}, s32[]{:T(128)}) %tuple.77), condition=%wide.region_4.0_spmd, body=%wide.region_3.0_spmd.sunk | while | flops 1208156160 | bytes 6553701 | solution.py:85
  4.5 5.8 %collective-permute-start = (f32[512,384]{1,0:T(8,128)}, f32[512,384]{1,0:T(8,128)}, u32[]{:S(2)}, u32[]{:S(2)}) collective-permute-start(f32[512,384]{1,0:T(8,128)} %get-tuple-element.274), channel_id=1, source_target_pairs={{0,4},{4,8},{8,12},{1,5},{5,9},{9,13},{2,6},{6,10},{10,14},{3,7},{... | collective-permute-start | bytes 2359304 | tf_op jit(solution)/shard_map/while/body/eval_jaxpr/ppermute | solution.py:13
  10.3 16.2 %collective-permute-done = f32[512,384]{1,0:T(8,128)} collective-permute-done((f32[512,384]{1,0:T(8,128)}, f32[512,384]{1,0:T(8,128)}, u32[]{:S(2)}, u32[]{:S(2)}) %collective-permute-start) | collective-permute-done | bytes 786464 | tf_op jit(solution)/shard_map/while/body/eval_jaxpr/ppermute | solution.py:13
  26.6 3.8 %convolution_subtract_fusion.2 = f32[512,384]{1,0:T(8,128)} fusion(f32[512,384]{1,0:T(8,128)S(1)} %get-tuple-element.281, f32[512,512]{1,0:T(8,128)S(1)} %get-tuple-element.280, f32[512,384]{1,0:T(8,128)} %collective-permute-done), kind=kOutput, calls=%fused_computation.2.clone.1 | convolution fusion | flops 1208156160 | bytes 3407872 | tf_op jit(solution)/shard_map/while/body/eval_jaxpr/dot_general | solution.py:17
  30.4 5.3 %collective-permute-start = (f32[512,384]{1,0:T(8,128)}, f32[512,384]{1,0:T(8,128)}, u32[]{:S(2)}, u32[]{:S(2)}) collective-permute-start(f32[512,384]{1,0:T(8,128)} %get-tuple-element.274), channel_id=1, source_target_pairs={{0,4},{4,8},{8,12},{1,5},{5,9},{9,13},{2,6},{6,10},{10,14},{3,7},{... | collective-permute-start | bytes 2359304 | tf_op jit(solution)/shard_map/while/body/eval_jaxpr/ppermute | solution.py:13
  35.7 15.4 %collective-permute-done = f32[512,384]{1,0:T(8,128)} collective-permute-done((f32[512,384]{1,0:T(8,128)}, f32[512,384]{1,0:T(8,128)}, u32[]{:S(2)}, u32[]{:S(2)}) %collective-permute-start) | collective-permute-done | bytes 786464 | tf_op jit(solution)/shard_map/while/body/eval_jaxpr/ppermute | solution.py:13
  51.0 3.8 %convolution_subtract_fusion.2 = f32[512,384]{1,0:T(8,128)} fusion(f32[512,384]{1,0:T(8,128)S(1)} %get-tuple-element.281, f32[512,512]{1,0:T(8,128)S(1)} %get-tuple-element.280, f32[512,384]{1,0:T(8,128)} %collective-permute-done), kind=kOutput, calls=%fused_computation.2.clone.1 | convolution fusion | flops 1208156160 | bytes 3407872 | tf_op jit(solution)/shard_map/while/body/eval_jaxpr/dot_general | solution.py:17
  54.9 5.3 %collective-permute-start = (f32[512,384]{1,0:T(8,128)}, f32[512,384]{1,0:T(8,128)}, u32[]{:S(2)}, u32[]{:S(2)}) collective-permute-start(f32[512,384]{1,0:T(8,128)} %get-tuple-element.274), channel_id=1, source_target_pairs={{0,4},{4,8},{8,12},{1,5},{5,9},{9,13},{2,6},{6,10},{10,14},{3,7},{... | collective-permute-start | bytes 2359304 | tf_op jit(solution)/shard_map/while/body/eval_jaxpr/ppermute | solution.py:13
  60.1 14.4 %collective-permute-done = f32[512,384]{1,0:T(8,128)} collective-permute-done((f32[512,384]{1,0:T(8,128)}, f32[512,384]{1,0:T(8,128)}, u32[]{:S(2)}, u32[]{:S(2)}) %collective-permute-start) | collective-permute-done | bytes 786464 | tf_op jit(solution)/shard_map/while/body/eval_jaxpr/ppermute | solution.py:13
  74.5 3.8 %convolution_subtract_fusion.2 = f32[512,384]{1,0:T(8,128)} fusion(f32[512,384]{1,0:T(8,128)S(1)} %get-tuple-element.281, f32[512,512]{1,0:T(8,128)S(1)} %get-tuple-element.280, f32[512,384]{1,0:T(8,128)} %collective-permute-done), kind=kOutput, calls=%fused_computation.2.clone.1 | convolution fusion | flops 1208156160 | bytes 3407872 | tf_op jit(solution)/shard_map/while/body/eval_jaxpr/dot_general | solution.py:17
  78.4 4.7 %convolution_bitcast_fusion = f32[512,384]{0,1:T(8,128)} fusion(f32[512,384]{1,0:T(8,128)} %get-tuple-element.98, f32[512,512]{1,0:T(8,128)S(1)} %copy-done), kind=kOutput, calls=%fused_computation.8 | convolution fusion | flops 1207959552 | bytes 2621440 | tf_op jit(solution)/shard_map/dot_general | solution.py:17
  83.1 1.4 copy.34
  85.4 72.7 %while.33 = (s32[]{:T(128)}, f32[512,384]{1,0:T(8,128)}, f32[512,512]{1,0:T(8,128)S(1)}, f32[512,384]{1,0:T(8,128)S(1)}, s32[]{:T(128)}) while((s32[]{:T(128)}, f32[512,384]{1,0:T(8,128)}, f32[512,512]{1,0:T(8,128)S(1)}, f32[512,384]{1,0:T(8,128)S(1)}, s32[]{:T(128)}) %tuple.78), condition=%wide.region_6.7_spmd, body=%wide.region_5.0_spmd.sunk | while | flops 1208156160 | bytes 8126565 | solution.py:92
  85.4 3.8 %fusion.37 = f32[512,384]{1,0:T(8,128)} fusion(f32[512,512]{1,0:T(8,128)S(1)} %get-tuple-element.295, f32[512,384]{1,0:T(8,128)} %get-tuple-element.289), kind=kOutput, calls=%fused_computation.57.clone.1 | convolution fusion | flops 1207959552 | bytes 2621440 | tf_op jit(solution)/shard_map/while/body/eval_jaxpr/dot_general | solution.py:17
  90.5 18.2 %collective-permute-done.1 = f32[512,384]{1,0:T(8,128)} collective-permute-done((f32[512,384]{1,0:T(8,128)}, f32[512,384]{1,0:T(8,128)}, u32[]{:S(2)}, u32[]{:S(2)}) %collective-permute-start.1) | collective-permute-done | bytes 786464 | tf_op jit(solution)/shard_map/while/body/eval_jaxpr/ppermute | solution.py:13
  108.7 2.1 sub.95
  110.8 3.8 %fusion.37 = f32[512,384]{1,0:T(8,128)} fusion(f32[512,512]{1,0:T(8,128)S(1)} %get-tuple-element.295, f32[512,384]{1,0:T(8,128)} %get-tuple-element.289), kind=kOutput, calls=%fused_computation.57.clone.1 | convolution fusion | flops 1207959552 | bytes 2621440 | tf_op jit(solution)/shard_map/while/body/eval_jaxpr/dot_general | solution.py:17
  116.0 16.8 %collective-permute-done.1 = f32[512,384]{1,0:T(8,128)} collective-permute-done((f32[512,384]{1,0:T(8,128)}, f32[512,384]{1,0:T(8,128)}, u32[]{:S(2)}, u32[]{:S(2)}) %collective-permute-start.1) | collective-permute-done | bytes 786464 | tf_op jit(solution)/shard_map/while/body/eval_jaxpr/ppermute | solution.py:13
  132.8 2.1 sub.95
  134.9 3.8 %fusion.37 = f32[512,384]{1,0:T(8,128)} fusion(f32[512,512]{1,0:T(8,128)S(1)} %get-tuple-element.295, f32[512,384]{1,0:T(8,128)} %get-tuple-element.289), kind=kOutput, calls=%fused_computation.57.clone.1 | convolution fusion | flops 1207959552 | bytes 2621440 | tf_op jit(solution)/shard_map/while/body/eval_jaxpr/dot_general | solution.py:17
  140.0 15.9 %collective-permute-done.1 = f32[512,384]{1,0:T(8,128)} collective-permute-done((f32[512,384]{1,0:T(8,128)}, f32[512,384]{1,0:T(8,128)}, u32[]{:S(2)}, u32[]{:S(2)}) %collective-permute-start.1) | collective-permute-done | bytes 786464 | tf_op jit(solution)/shard_map/while/body/eval_jaxpr/ppermute | solution.py:13
  155.9 2.1 sub.95
  158.0 1.4 copy.36
  159.4 4.5 %convolution_bitcast_fusion.1 = f32[2,3,128]{1,0,2:T(2,128)S(1)} fusion(f32[512,3,128]{0,2,1:T(8,128)S(1)} %bitcast.81, f32[512,2,128]{0,2,1:T(8,128)S(1)} %convert_subtract_fusion), kind=kOutput, calls=%fused_computation.9 | convolution fusion | flops 4718592 | bytes 1313792 | tf_op jit(solution)/shard_map/bit,bct->ict/dot_general | solution.py:94
  163.9 19.6 %psum.7 = f32[2,3,128]{1,0,2:T(2,128)S(1)} all-reduce(f32[2,3,128]{1,0,2:T(2,128)S(1)} %convolution_bitcast_fusion.1), channel_id=1, replica_groups=mesh['groups'=2,'front'=4,'batch'=2,'line'=2] {'front'}, use_global_device_ids=true, to_apply=%region_7.8 | all-reduce | flops 768 | bytes 6144 | tf_op jit(solution)/shard_map/psum | solution.py:97
  183.5 2.2 slice_reduce_fusion.2
  186.2 1.3 collective-permute-start.2
  189.1 5.4 %collective-permute-done.2 = f32[512,128]{1,0:T(8,128)S(1)} collective-permute-done((f32[512,128]{1,0:T(8,128)S(1)}, f32[512,128]{1,0:T(8,128)S(1)}, u32[]{:S(2)}, u32[]{:S(2)}) %collective-permute-start.2) | collective-permute-done | bytes 262176 | tf_op jit(solution)/shard_map/ppermute | solution.py:13
  196.7 1.9 fusion
  198.6 3.5 %all-to-all-start = ((f32[8,128,128]{2,1,0:T(8,128)}), f32[8,128,128]{2,1,0:T(8,128)S(1)}, u32[]{:S(2)}, u32[]{:S(2)}) async-start(f32[8,128,128]{2,1,0:T(8,128)} %bitcast.13), calls=%async_computation | async-start | bytes 1048576 | tf_op jit(solution)/shard_map/all_to_all | solution.py:116
  202.1 15.2 %all-to-all-done = f32[8,128,128]{2,1,0:T(8,128)S(1)} async-done(((f32[8,128,128]{2,1,0:T(8,128)}), f32[8,128,128]{2,1,0:T(8,128)S(1)}, u32[]{:S(2)}, u32[]{:S(2)}) %all-to-all-start) | async-done | bytes 524320 | tf_op jit(solution)/shard_map/all_to_all | solution.py:116
  217.4 25.2 %while.34 = (s32[]{:T(128)}, f32[128,128]{1,0:T(8,128)S(1)}, f32[32,32,128]{2,1,0:T(8,128)S(1)}, f32[128]{0:T(128)S(1)}, f32[128]{0:T(128)S(1)}, /*index=5*/f32[1,1,128]{2,1,0:T(1,128)S(1)}, s32[]{:T(128)}, s32[]{:T(128)}) while((s32[]{:T(128)}, f32[128,128]{1,0:T(8,128)S(1)}, f32[32,32,128]{2,1,0:T(8,128)S(1)}, ...), condition=%wide.region_10.11_spmd.clone, body=%wide.region_8.10_spmd.clone.sunk | while | flops 2113539 | bytes 312931 | solution.py:125
  (152 shorter events, 37.3 us)
Async XLA Ops:
  0.6 77.8 %copy-start = (f32[512,512]{1,0:T(8,128)S(1)}, f32[512,512]{1,0:T(8,128)}, u32[]{:S(2)}) copy-start(f32[512,512]{1,0:T(8,128)} %param.24) | copy-start | bytes 3145732
  3.0 1.5 copy-start.1
  4.5 22.0 %collective-permute-start = (f32[512,384]{1,0:T(8,128)}, f32[512,384]{1,0:T(8,128)}, u32[]{:S(2)}, u32[]{:S(2)}) collective-permute-start(f32[512,384]{1,0:T(8,128)} %get-tuple-element.274), channel_id=1, source_target_pairs={{0,4},{4,8},{8,12},{1,5},{5,9},{9,13},{2,6},{6,10},{10,14},{3,7},{... | collective-permute-start | bytes 2359304 | tf_op jit(solution)/shard_map/while/body/eval_jaxpr/ppermute | solution.py:13
  30.4 20.6 %collective-permute-start = (f32[512,384]{1,0:T(8,128)}, f32[512,384]{1,0:T(8,128)}, u32[]{:S(2)}, u32[]{:S(2)}) collective-permute-start(f32[512,384]{1,0:T(8,128)} %get-tuple-element.274), channel_id=1, source_target_pairs={{0,4},{4,8},{8,12},{1,5},{5,9},{9,13},{2,6},{6,10},{10,14},{3,7},{... | collective-permute-start | bytes 2359304 | tf_op jit(solution)/shard_map/while/body/eval_jaxpr/ppermute | solution.py:13
  54.9 19.7 %collective-permute-start = (f32[512,384]{1,0:T(8,128)}, f32[512,384]{1,0:T(8,128)}, u32[]{:S(2)}, u32[]{:S(2)}) collective-permute-start(f32[512,384]{1,0:T(8,128)} %get-tuple-element.274), channel_id=1, source_target_pairs={{0,4},{4,8},{8,12},{1,5},{5,9},{9,13},{2,6},{6,10},{10,14},{3,7},{... | collective-permute-start | bytes 2359304 | tf_op jit(solution)/shard_map/while/body/eval_jaxpr/ppermute | solution.py:13
  89.2 19.5 %collective-permute-start.1 = (f32[512,384]{1,0:T(8,128)}, f32[512,384]{1,0:T(8,128)}, u32[]{:S(2)}, u32[]{:S(2)}) collective-permute-start(f32[512,384]{1,0:T(8,128)} %fusion.37), channel_id=1, source_target_pairs={{4,0},{8,4},{12,8},{5,1},{9,5},{13,9},{6,2},{10,6},{14,10},{7,3},{... | collective-permute-start | bytes 2359304 | tf_op jit(solution)/shard_map/while/body/eval_jaxpr/ppermute | solution.py:13
  114.7 18.1 %collective-permute-start.1 = (f32[512,384]{1,0:T(8,128)}, f32[512,384]{1,0:T(8,128)}, u32[]{:S(2)}, u32[]{:S(2)}) collective-permute-start(f32[512,384]{1,0:T(8,128)} %fusion.37), channel_id=1, source_target_pairs={{4,0},{8,4},{12,8},{5,1},{9,5},{13,9},{6,2},{10,6},{14,10},{7,3},{... | collective-permute-start | bytes 2359304 | tf_op jit(solution)/shard_map/while/body/eval_jaxpr/ppermute | solution.py:13
  138.7 17.2 %collective-permute-start.1 = (f32[512,384]{1,0:T(8,128)}, f32[512,384]{1,0:T(8,128)}, u32[]{:S(2)}, u32[]{:S(2)}) collective-permute-start(f32[512,384]{1,0:T(8,128)} %fusion.37), channel_id=1, source_target_pairs={{4,0},{8,4},{12,8},{5,1},{9,5},{13,9},{6,2},{10,6},{14,10},{7,3},{... | collective-permute-start | bytes 2359304 | tf_op jit(solution)/shard_map/while/body/eval_jaxpr/ppermute | solution.py:13
  163.9 21.8 %copy-start.8 = (f32[2,128]{1,0:T(2,128)S(1)}, f32[2,128]{1,0:T(2,128)}, u32[]{:S(2)}) copy-start(f32[2,128]{1,0:T(2,128)} %param.22) | copy-start | bytes 3076
  185.9 1.7 copy-start.6
  185.9 1.7 copy-start.7
  185.9 1.7 copy-start.4
  186.2 9.4 %copy-start.2 = (f32[512,128]{1,0:T(8,128)}, f32[512,128]{1,0:T(8,128)S(1)}, u32[]{:S(2)}) copy-start(f32[512,128]{1,0:T(8,128)S(1)} %bitcast_subtract_fusion) | copy-start | bytes 786436
  186.2 8.3 %collective-permute-start.2 = (f32[512,128]{1,0:T(8,128)S(1)}, f32[512,128]{1,0:T(8,128)S(1)}, u32[]{:S(2)}, u32[]{:S(2)}) collective-permute-start(f32[512,128]{1,0:T(8,128)S(1)} %bitcast_subtract_fusion), channel_id=1, source_target_pairs={{4,0},{8,4},{12,8},{5,1},{9,5},{13,9},{6,2},{10,6},{14,10},{7,3},{... | collective-permute-start | bytes 786440 | tf_op jit(solution)/shard_map/ppermute | solution.py:13
  195.6 1.1 copy-start.5
  196.7 5.5 %copy-start.10 = (f32[128]{0:T(128)S(1)}, f32[128]{0:T(128)}, u32[]{:S(2)}) copy-start(f32[128]{0:T(128)} %param.30) | copy-start | bytes 1540
  196.7 20.7 %copy-start.9 = (f32[128]{0:T(128)S(1)}, f32[128]{0:T(128)}, u32[]{:S(2)}) copy-start(f32[128]{0:T(128)} %param.29) | copy-start | bytes 1540
  198.6 18.8 %all-to-all-start = ((f32[8,128,128]{2,1,0:T(8,128)}), f32[8,128,128]{2,1,0:T(8,128)S(1)}, u32[]{:S(2)}, u32[]{:S(2)}) async-start(f32[8,128,128]{2,1,0:T(8,128)} %bitcast.13), calls=%async_computation | async-start | bytes 1048576 | tf_op jit(solution)/shard_map/all_to_all | solution.py:116
  217.4 25.2 %copy-start.3 = (bf16[128,128]{1,0:T(8,128)(2,1)S(1)}, bf16[128,128]{1,0:T(8,128)(2,1)}, u32[]{:S(2)}) copy-start(bf16[128,128]{1,0:T(8,128)(2,1)} %param.31) | copy-start | bytes 98308
where the time goes:
time: 244 us; the launch traced here: 243 us
  waiting for transfers between devices  118 us (48%)
  matrix products  34.9 us (14%)
  other arithmetic  32.3 us (13%)
  starting transfers between devices  24.9 us (10%)
  blocking collectives  19.6 us (8%)
  local copies, waits for them, and re-layouts  11.7 us (5%)
    ppermute x7, waiting for transfers between devices, from_behind(): return lax.ppermute(value, axis, pairs)  102 us
    dot_general x8, matrix products, product(): jnp.dot(operand, against, precision=lax.Precision.HIGHEST, preferred_elem...  29.7 us
    reduce_sum x32, other arithmetic, accumulate(): jnp.sum(centered_tanh(slot_block, in_weight, in_bias), axis=0)  23 us
    ppermute x7, starting transfers between devices, from_behind(): return lax.ppermute(value, axis, pairs)  21.5 us
    psum x1, blocking collectives, body(): terms = lax.psum(local_terms, 'front')  19.6 us
    all_to_all x1, waiting for transfers between devices, body(): lax.all_to_all(outgoing, ('front', 'line'), split_axis=0, concat_axis=0,...  15.2 us
    sub x3, other arithmetic, upper_step(): return pivoted - arrived  6.31 us
  transfers between devices with their start and end apart: 8, of which 8 were waited for; matrix products, arithmetic and copies ran while one was open for 1% of the time, Pallas kernels for 0%

commit v1 on v0

--- a/solution.py
+++ b/solution.py
@@ -94,7 +94,8 @@
     local_terms = jnp.einsum(
         "bit,bct->ict", incidence, solved_cols, precision=lax.Precision.HIGHEST
     )
-    terms = lax.psum(local_terms, "front")
+    parts = lax.all_gather(local_terms, "front")
+    terms = jnp.sum(parts, axis=0)
     weights = capacitance_solve(terms, switch_susc)
     angles = solved_cols[:, 0, :] - jnp.einsum(
         "bit,it->bt", solved_cols[:, 1:, :], weights, precision=lax.Precision.HIGHEST

time: 244 us -> 236 us (0.967)
  blocking collectives: 19.6 us -> 13.1 us
    psum x1 -> x0, blocking collectives: 19.6 us -> none  [body(): terms = lax.psum(local_terms, 'front')]
    all_gather x0 -> x1, blocking collectives: none -> 13.1 us  [body(): parts = lax.all_gather(local_terms, 'front')]
where the time goes in v1:
time: 236 us; the launch traced here: 235 us
  waiting for transfers between devices  117 us (50%)
  matrix products  34.9 us (15%)
  other arithmetic  32.3 us (14%)
  starting transfers between devices  25.1 us (11%)
  blocking collectives  13.1 us (6%)
  local copies, waits for them, and re-layouts  9.57 us (4%)
    ppermute x7, waiting for transfers between devices, from_behind(): return lax.ppermute(value, axis, pairs)  102 us
    dot_general x8, matrix products, product(): jnp.dot(operand, against, precision=lax.Precision.HIGHEST, preferred_elem...  29.7 us
    reduce_sum x32, other arithmetic, accumulate(): jnp.sum(centered_tanh(slot_block, in_weight, in_bias), axis=0)  23 us
    ppermute x7, starting transfers between devices, from_behind(): return lax.ppermute(value, axis, pairs)  21.6 us
    all_to_all x1, waiting for transfers between devices, body(): lax.all_to_all(outgoing, ('front', 'line'), split_axis=0, concat_axis=0,...  15.2 us
    all_gather x1, blocking collectives, body(): parts = lax.all_gather(local_terms, 'front')  13.1 us
    sub x3, other arithmetic, upper_step(): return pivoted - arrived  6.33 us
  transfers between devices with their start and end apart: 8, of which 8 were waited for; matrix products, arithmetic and copies ran while one was open for 1% of the time, Pallas kernels for 0%

profile of v1, /device:TPU:0, one launch (start us, length us, event | category | flops | bytes accessed | tf_op | source)
XLA Modules:
  0.0 234.9 jit_solution(1498242732047019790)
XLA Ops:
  4.5 73.8 %while.32 = (s32[]{:T(128)}, f32[512,384]{1,0:T(8,128)}, f32[512,512]{1,0:T(8,128)S(1)}, f32[512,384]{1,0:T(8,128)S(1)}, s32[]{:T(128)}) while((s32[]{:T(128)}, f32[512,384]{1,0:T(8,128)}, f32[512,512]{1,0:T(8,128)S(1)}, f32[512,384]{1,0:T(8,128)S(1)}, s32[]{:T(128)}) %tuple.77), condition=%wide.region_4.0_spmd, body=%wide.region_3.0_spmd.sunk | while | flops 1208156160 | bytes 6553701 | solution.py:85
  4.5 5.8 %collective-permute-start = (f32[512,384]{1,0:T(8,128)}, f32[512,384]{1,0:T(8,128)}, u32[]{:S(2)}, u32[]{:S(2)}) collective-permute-start(f32[512,384]{1,0:T(8,128)} %get-tuple-element.285), channel_id=1, source_target_pairs={{0,4},{4,8},{8,12},{1,5},{5,9},{9,13},{2,6},{6,10},{10,14},{3,7},{... | collective-permute-start | bytes 2359304 | tf_op jit(solution)/shard_map/while/body/eval_jaxpr/ppermute | solution.py:13
  10.3 16.2 %collective-permute-done = f32[512,384]{1,0:T(8,128)} collective-permute-done((f32[512,384]{1,0:T(8,128)}, f32[512,384]{1,0:T(8,128)}, u32[]{:S(2)}, u32[]{:S(2)}) %collective-permute-start) | collective-permute-done | bytes 786464 | tf_op jit(solution)/shard_map/while/body/eval_jaxpr/ppermute | solution.py:13
  26.6 3.8 %convolution_subtract_fusion.2 = f32[512,384]{1,0:T(8,128)} fusion(f32[512,384]{1,0:T(8,128)S(1)} %get-tuple-element.292, f32[512,512]{1,0:T(8,128)S(1)} %get-tuple-element.291, f32[512,384]{1,0:T(8,128)} %collective-permute-done), kind=kOutput, calls=%fused_computation.2.clone.1 | convolution fusion | flops 1208156160 | bytes 3407872 | tf_op jit(solution)/shard_map/while/body/eval_jaxpr/dot_general | solution.py:17
  30.4 5.3 %collective-permute-start = (f32[512,384]{1,0:T(8,128)}, f32[512,384]{1,0:T(8,128)}, u32[]{:S(2)}, u32[]{:S(2)}) collective-permute-start(f32[512,384]{1,0:T(8,128)} %get-tuple-element.285), channel_id=1, source_target_pairs={{0,4},{4,8},{8,12},{1,5},{5,9},{9,13},{2,6},{6,10},{10,14},{3,7},{... | collective-permute-start | bytes 2359304 | tf_op jit(solution)/shard_map/while/body/eval_jaxpr/ppermute | solution.py:13
  35.7 15.3 %collective-permute-done = f32[512,384]{1,0:T(8,128)} collective-permute-done((f32[512,384]{1,0:T(8,128)}, f32[512,384]{1,0:T(8,128)}, u32[]{:S(2)}, u32[]{:S(2)}) %collective-permute-start) | collective-permute-done | bytes 786464 | tf_op jit(solution)/shard_map/while/body/eval_jaxpr/ppermute | solution.py:13
  51.0 3.8 %convolution_subtract_fusion.2 = f32[512,384]{1,0:T(8,128)} fusion(f32[512,384]{1,0:T(8,128)S(1)} %get-tuple-element.292, f32[512,512]{1,0:T(8,128)S(1)} %get-tuple-element.291, f32[512,384]{1,0:T(8,128)} %collective-permute-done), kind=kOutput, calls=%fused_computation.2.clone.1 | convolution fusion | flops 1208156160 | bytes 3407872 | tf_op jit(solution)/shard_map/while/body/eval_jaxpr/dot_general | solution.py:17
  54.8 5.3 %collective-permute-start = (f32[512,384]{1,0:T(8,128)}, f32[512,384]{1,0:T(8,128)}, u32[]{:S(2)}, u32[]{:S(2)}) collective-permute-start(f32[512,384]{1,0:T(8,128)} %get-tuple-element.285), channel_id=1, source_target_pairs={{0,4},{4,8},{8,12},{1,5},{5,9},{9,13},{2,6},{6,10},{10,14},{3,7},{... | collective-permute-start | bytes 2359304 | tf_op jit(solution)/shard_map/while/body/eval_jaxpr/ppermute | solution.py:13
  60.1 14.4 %collective-permute-done = f32[512,384]{1,0:T(8,128)} collective-permute-done((f32[512,384]{1,0:T(8,128)}, f32[512,384]{1,0:T(8,128)}, u32[]{:S(2)}, u32[]{:S(2)}) %collective-permute-start) | collective-permute-done | bytes 786464 | tf_op jit(solution)/shard_map/while/body/eval_jaxpr/ppermute | solution.py:13
  74.5 3.8 %convolution_subtract_fusion.2 = f32[512,384]{1,0:T(8,128)} fusion(f32[512,384]{1,0:T(8,128)S(1)} %get-tuple-element.292, f32[512,512]{1,0:T(8,128)S(1)} %get-tuple-element.291, f32[512,384]{1,0:T(8,128)} %collective-permute-done), kind=kOutput, calls=%fused_computation.2.clone.1 | convolution fusion | flops 1208156160 | bytes 3407872 | tf_op jit(solution)/shard_map/while/body/eval_jaxpr/dot_general | solution.py:17
  78.4 4.7 %convolution_bitcast_fusion = f32[512,384]{0,1:T(8,128)} fusion(f32[512,384]{1,0:T(8,128)} %get-tuple-element.98, f32[512,512]{1,0:T(8,128)S(1)} %copy-done), kind=kOutput, calls=%fused_computation.8 | convolution fusion | flops 1207959552 | bytes 2621440 | tf_op jit(solution)/shard_map/dot_general | solution.py:17
  83.0 1.4 copy.56
  85.3 72.7 %while.33 = (s32[]{:T(128)}, f32[512,384]{1,0:T(8,128)}, f32[512,512]{1,0:T(8,128)S(1)}, f32[512,384]{1,0:T(8,128)S(1)}, s32[]{:T(128)}) while((s32[]{:T(128)}, f32[512,384]{1,0:T(8,128)}, f32[512,512]{1,0:T(8,128)S(1)}, f32[512,384]{1,0:T(8,128)S(1)}, s32[]{:T(128)}) %tuple.78), condition=%wide.region_6.7_spmd, body=%wide.region_5.0_spmd.sunk | while | flops 1208156160 | bytes 8126565 | solution.py:92
  85.3 3.8 %fusion.40 = f32[512,384]{1,0:T(8,128)} fusion(f32[512,512]{1,0:T(8,128)S(1)} %get-tuple-element.306, f32[512,384]{1,0:T(8,128)} %get-tuple-element.300), kind=kOutput, calls=%fused_computation.57.clone.1 | convolution fusion | flops 1207959552 | bytes 2621440 | tf_op jit(solution)/shard_map/while/body/eval_jaxpr/dot_general | solution.py:17
  89.2 1.3 collective-permute-start.1
  90.5 18.2 %collective-permute-done.1 = f32[512,384]{1,0:T(8,128)} collective-permute-done((f32[512,384]{1,0:T(8,128)}, f32[512,384]{1,0:T(8,128)}, u32[]{:S(2)}, u32[]{:S(2)}) %collective-permute-start.1) | collective-permute-done | bytes 786464 | tf_op jit(solution)/shard_map/while/body/eval_jaxpr/ppermute | solution.py:13
  108.7 2.1 sub.95
  110.8 3.8 %fusion.40 = f32[512,384]{1,0:T(8,128)} fusion(f32[512,512]{1,0:T(8,128)S(1)} %get-tuple-element.306, f32[512,384]{1,0:T(8,128)} %get-tuple-element.300), kind=kOutput, calls=%fused_computation.57.clone.1 | convolution fusion | flops 1207959552 | bytes 2621440 | tf_op jit(solution)/shard_map/while/body/eval_jaxpr/dot_general | solution.py:17
  116.0 16.8 %collective-permute-done.1 = f32[512,384]{1,0:T(8,128)} collective-permute-done((f32[512,384]{1,0:T(8,128)}, f32[512,384]{1,0:T(8,128)}, u32[]{:S(2)}, u32[]{:S(2)}) %collective-permute-start.1) | collective-permute-done | bytes 786464 | tf_op jit(solution)/shard_map/while/body/eval_jaxpr/ppermute | solution.py:13
  132.8 2.1 sub.95
  134.9 3.8 %fusion.40 = f32[512,384]{1,0:T(8,128)} fusion(f32[512,512]{1,0:T(8,128)S(1)} %get-tuple-element.306, f32[512,384]{1,0:T(8,128)} %get-tuple-element.300), kind=kOutput, calls=%fused_computation.57.clone.1 | convolution fusion | flops 1207959552 | bytes 2621440 | tf_op jit(solution)/shard_map/while/body/eval_jaxpr/dot_general | solution.py:17
  140.0 15.9 %collective-permute-done.1 = f32[512,384]{1,0:T(8,128)} collective-permute-done((f32[512,384]{1,0:T(8,128)}, f32[512,384]{1,0:T(8,128)}, u32[]{:S(2)}, u32[]{:S(2)}) %collective-permute-start.1) | collective-permute-done | bytes 786464 | tf_op jit(solution)/shard_map/while/body/eval_jaxpr/ppermute | solution.py:13
  156.0 2.1 sub.95
  158.1 1.4 copy.58
  159.5 4.5 %convolution_bitcast_fusion.1 = f32[2,3,128]{1,0,2:T(2,128)S(1)} fusion(f32[512,3,128]{0,2,1:T(8,128)S(1)} %bitcast.102, f32[512,2,128]{0,2,1:T(8,128)S(1)} %convert_subtract_fusion), kind=kOutput, calls=%fused_computation.9 | convolution fusion | flops 4718592 | bytes 1313792 | tf_op jit(solution)/shard_map/bit,bct->ict/dot_general | solution.py:94
  164.1 13.1 %all-gather = f32[8,3,128]{2,1,0:T(4,128)S(1)} all-gather(f32[2,3,128]{2,1,0:T(4,128)S(1)} %copy.62), channel_id=2, replica_groups=mesh['groups'=2,'front'=4,'batch'=2,'line'=2] {'front'}, dimensions={0}, use_global_device_ids=true | all-gather | bytes 15360 | tf_op jit(solution)/shard_map/all_gather | solution.py:97
  177.8 1.5 collective-permute-start.2
  180.8 5.2 %collective-permute-done.2 = f32[512,128]{1,0:T(8,128)S(1)} collective-permute-done((f32[512,128]{1,0:T(8,128)S(1)}, f32[512,128]{1,0:T(8,128)S(1)}, u32[]{:S(2)}, u32[]{:S(2)}) %collective-permute-start.2) | collective-permute-done | bytes 262176 | tf_op jit(solution)/shard_map/ppermute | solution.py:13
  188.2 1.9 fusion
  190.1 3.5 %all-to-all-start = ((f32[8,128,128]{2,1,0:T(8,128)}), f32[8,128,128]{2,1,0:T(8,128)S(1)}, u32[]{:S(2)}, u32[]{:S(2)}) async-start(f32[8,128,128]{2,1,0:T(8,128)} %bitcast.14), calls=%async_computation | async-start | bytes 1048576 | tf_op jit(solution)/shard_map/all_to_all | solution.py:117
  193.7 15.2 %all-to-all-done = f32[8,128,128]{2,1,0:T(8,128)S(1)} async-done(((f32[8,128,128]{2,1,0:T(8,128)}), f32[8,128,128]{2,1,0:T(8,128)S(1)}, u32[]{:S(2)}, u32[]{:S(2)}) %all-to-all-start) | async-done | bytes 524320 | tf_op jit(solution)/shard_map/all_to_all | solution.py:117
  208.9 25.2 %while.34 = (s32[]{:T(128)}, f32[128,128]{1,0:T(8,128)S(1)}, f32[32,32,128]{2,1,0:T(8,128)S(1)}, f32[128]{0:T(128)S(1)}, f32[128]{0:T(128)S(1)}, /*index=5*/f32[1,1,128]{2,1,0:T(1,128)S(1)}, s32[]{:T(128)}, s32[]{:T(128)}) while((s32[]{:T(128)}, f32[128,128]{1,0:T(8,128)S(1)}, f32[32,32,128]{2,1,0:T(8,128)S(1)}, ...), condition=%wide.region_10.11_spmd.clone, body=%wide.region_8.10_spmd.clone.sunk | while | flops 2113539 | bytes 312931 | solution.py:126
  (153 shorter events, 36.1 us)
Async XLA Ops:
  0.6 77.7 %copy-start = (f32[512,512]{1,0:T(8,128)S(1)}, f32[512,512]{1,0:T(8,128)}, u32[]{:S(2)}) copy-start(f32[512,512]{1,0:T(8,128)} %param.24) | copy-start | bytes 3145732
  3.0 1.5 copy-start.1
  4.5 22.0 %collective-permute-start = (f32[512,384]{1,0:T(8,128)}, f32[512,384]{1,0:T(8,128)}, u32[]{:S(2)}, u32[]{:S(2)}) collective-permute-start(f32[512,384]{1,0:T(8,128)} %get-tuple-element.285), channel_id=1, source_target_pairs={{0,4},{4,8},{8,12},{1,5},{5,9},{9,13},{2,6},{6,10},{10,14},{3,7},{... | collective-permute-start | bytes 2359304 | tf_op jit(solution)/shard_map/while/body/eval_jaxpr/ppermute | solution.py:13
  30.4 20.6 %collective-permute-start = (f32[512,384]{1,0:T(8,128)}, f32[512,384]{1,0:T(8,128)}, u32[]{:S(2)}, u32[]{:S(2)}) collective-permute-start(f32[512,384]{1,0:T(8,128)} %get-tuple-element.285), channel_id=1, source_target_pairs={{0,4},{4,8},{8,12},{1,5},{5,9},{9,13},{2,6},{6,10},{10,14},{3,7},{... | collective-permute-start | bytes 2359304 | tf_op jit(solution)/shard_map/while/body/eval_jaxpr/ppermute | solution.py:13
  54.8 19.7 %collective-permute-start = (f32[512,384]{1,0:T(8,128)}, f32[512,384]{1,0:T(8,128)}, u32[]{:S(2)}, u32[]{:S(2)}) collective-permute-start(f32[512,384]{1,0:T(8,128)} %get-tuple-element.285), channel_id=1, source_target_pairs={{0,4},{4,8},{8,12},{1,5},{5,9},{9,13},{2,6},{6,10},{10,14},{3,7},{... | collective-permute-start | bytes 2359304 | tf_op jit(solution)/shard_map/while/body/eval_jaxpr/ppermute | solution.py:13
  89.2 19.5 %collective-permute-start.1 = (f32[512,384]{1,0:T(8,128)}, f32[512,384]{1,0:T(8,128)}, u32[]{:S(2)}, u32[]{:S(2)}) collective-permute-start(f32[512,384]{1,0:T(8,128)} %fusion.40), channel_id=1, source_target_pairs={{4,0},{8,4},{12,8},{5,1},{9,5},{13,9},{6,2},{10,6},{14,10},{7,3},{... | collective-permute-start | bytes 2359304 | tf_op jit(solution)/shard_map/while/body/eval_jaxpr/ppermute | solution.py:13
  114.7 18.1 %collective-permute-start.1 = (f32[512,384]{1,0:T(8,128)}, f32[512,384]{1,0:T(8,128)}, u32[]{:S(2)}, u32[]{:S(2)}) collective-permute-start(f32[512,384]{1,0:T(8,128)} %fusion.40), channel_id=1, source_target_pairs={{4,0},{8,4},{12,8},{5,1},{9,5},{13,9},{6,2},{10,6},{14,10},{7,3},{... | collective-permute-start | bytes 2359304 | tf_op jit(solution)/shard_map/while/body/eval_jaxpr/ppermute | solution.py:13
  138.8 17.2 %collective-permute-start.1 = (f32[512,384]{1,0:T(8,128)}, f32[512,384]{1,0:T(8,128)}, u32[]{:S(2)}, u32[]{:S(2)}) collective-permute-start(f32[512,384]{1,0:T(8,128)} %fusion.40), channel_id=1, source_target_pairs={{4,0},{8,4},{12,8},{5,1},{9,5},{13,9},{6,2},{10,6},{14,10},{7,3},{... | collective-permute-start | bytes 2359304 | tf_op jit(solution)/shard_map/while/body/eval_jaxpr/ppermute | solution.py:13
  159.5 17.8 %copy-start.8 = (f32[2,128]{1,0:T(2,128)S(1)}, f32[2,128]{1,0:T(2,128)}, u32[]{:S(2)}) copy-start(f32[2,128]{1,0:T(2,128)} %param.22) | copy-start | bytes 3076
  177.4 1.8 copy-start.6
  177.4 1.8 copy-start.7
  177.4 1.9 copy-start.4
  177.7 9.4 %copy-start.2 = (f32[512,128]{1,0:T(8,128)}, f32[512,128]{1,0:T(8,128)S(1)}, u32[]{:S(2)}) copy-start(f32[512,128]{1,0:T(8,128)S(1)} %bitcast_subtract_fusion) | copy-start | bytes 786436
  177.8 8.3 %collective-permute-start.2 = (f32[512,128]{1,0:T(8,128)S(1)}, f32[512,128]{1,0:T(8,128)S(1)}, u32[]{:S(2)}, u32[]{:S(2)}) collective-permute-start(f32[512,128]{1,0:T(8,128)S(1)} %bitcast_subtract_fusion), channel_id=1, source_target_pairs={{4,0},{8,4},{12,8},{5,1},{9,5},{13,9},{6,2},{10,6},{14,10},{7,3},{... | collective-permute-start | bytes 786440 | tf_op jit(solution)/shard_map/ppermute | solution.py:13
  187.1 1.1 copy-start.5
  188.2 5.5 %copy-start.10 = (f32[128]{0:T(128)S(1)}, f32[128]{0:T(128)}, u32[]{:S(2)}) copy-start(f32[128]{0:T(128)} %param.30) | copy-start | bytes 1540
  188.2 20.7 %copy-start.9 = (f32[128]{0:T(128)S(1)}, f32[128]{0:T(128)}, u32[]{:S(2)}) copy-start(f32[128]{0:T(128)} %param.29) | copy-start | bytes 1540
  190.1 18.8 %all-to-all-start = ((f32[8,128,128]{2,1,0:T(8,128)}), f32[8,128,128]{2,1,0:T(8,128)S(1)}, u32[]{:S(2)}, u32[]{:S(2)}) async-start(f32[8,128,128]{2,1,0:T(8,128)} %bitcast.14), calls=%async_computation | async-start | bytes 1048576 | tf_op jit(solution)/shard_map/all_to_all | solution.py:117
  208.9 25.2 %copy-start.3 = (bf16[128,128]{1,0:T(8,128)(2,1)S(1)}, bf16[128,128]{1,0:T(8,128)(2,1)}, u32[]{:S(2)}) copy-start(bf16[128,128]{1,0:T(8,128)(2,1)} %param.31) | copy-start | bytes 98308
